TPU v7x, 32 devices: a whole 2x2x4 slice. The times are simulated.
32 devices in a mesh: dp: 4 (over z), expert: 2 (over core), tensor: 4 (over y, x).
Axes of the slice: x: 2, y: 2, z: 4, core: 2. Of those that a mesh axis runs over, the one named last changes fastest.
Arguments:
- tokens: bfloat16 [4096, 6144], P(('dp', 'expert'), 'tensor'), parts along dimension 0, may hold values from -6 to 6
- route_ids: int32 [4096, 2], P(('dp', 'expert')), parts along dimension 0, may hold values from 0 to 7, as said below
- route_gates: float32 [4096, 2], P(('dp', 'expert')), parts along dimension 0, may hold values from 0.2 to 1
- w_gate: bfloat16 [2, 6144, 2048], P('expert', None, 'tensor'), may hold values from -0.078125 to 0.078125
- w_up: bfloat16 [2, 6144, 2048], P('expert', None, 'tensor'), may hold values from -0.078125 to 0.078125
- w_down: bfloat16 [2, 2048, 6144], P('expert', 'tensor'), may hold values from -0.125 to 0.125
Outputs:
- mixed: bfloat16 [4096, 6144], P(('dp', 'expert'), 'tensor'), parts along dimension 0
There are 4 independent parts, one for each index of `dp`. A program takes and returns all parts, laid end to end along the dimension named above; an argument that names none is the same for every part. Nothing has to cross between parts.
Inputs may be any that keep to these rules, and one draw needn't show every extreme that they name: `route_ids`: in each aligned block of 512 rows (the rows of one expert index) every expert is named at most 256 times, and one expert below 2, the same in all blocks of a replica, is named exactly 256 times in every block. The 2 experts of a row differ.
All inputs are finite; a program needn't handle non-finite values.
Results may differ from a plain program's by a relative error of at most 0.0057.
Values may be sent and summed in bfloat16 or wider, within the bound.
A program may use at most 128 MiB of HBM per device.

v0:
```python
import jax
import jax.numpy as jnp
from jax import lax
from jax.sharding import PartitionSpec as P


def body(tokens, route_ids, route_gates, w_gate, w_up, w_down):
    tok_rows, width_dev = tokens.shape
    picks = route_ids.shape[1]
    n_source = lax.axis_size("expert")
    local_count = w_gate.shape[0]
    n_flight = n_source * local_count
    capacity = tok_rows // 2
    flat_ids = route_ids.reshape(-1)
    onehot = (flat_ids[:, None] == jnp.arange(n_flight, dtype=jnp.int32)[None, :]).astype(jnp.int32)
    earlier = jnp.cumsum(onehot, axis=0) - onehot
    position = jnp.sum(earlier * onehot, axis=1)
    in_window = flat_ids < n_flight
    slots = jnp.where(in_window, flat_ids * capacity + position, n_flight * capacity)
    repeated = jnp.repeat(tokens, picks, axis=0)
    buffer = (
        jnp.zeros((n_flight * capacity, width_dev), jnp.bfloat16)
        .at[slots]
        .set(repeated, mode="drop")
    )
    buffer = buffer.reshape(n_flight, capacity, width_dev)
    received = lax.all_to_all(buffer, "expert", split_axis=0, concat_axis=0, tiled=True)
    piece = lax.all_gather(received, "tensor", axis=2, tiled=True)
    columns = piece.shape[2]
    grouped = piece.reshape(n_source, local_count, capacity, columns)
    gate = jnp.einsum("secd,edf->secf", grouped, w_gate, preferred_element_type=jnp.float32)
    upper = jnp.einsum("secd,edf->secf", grouped, w_up, preferred_element_type=jnp.float32)
    gated = (jax.nn.silu(gate) * upper).astype(jnp.bfloat16)
    partial_out = jnp.einsum("secf,efd->secd", gated, w_down, preferred_element_type=jnp.float32)
    partial_out = partial_out.reshape(n_flight, capacity, partial_out.shape[3])
    summed = lax.psum_scatter(partial_out, "tensor", scatter_dimension=2, tiled=True)
    expert_out = summed.astype(jnp.bfloat16)
    back = lax.all_to_all(expert_out, "expert", split_axis=0, concat_axis=0, tiled=True)
    flat_back = back.reshape(n_flight * capacity, width_dev)
    picked = jnp.take(flat_back, slots, axis=0, mode="fill", fill_value=0).astype(jnp.float32)
    picked = picked.reshape(tok_rows, picks, width_dev)
    mixed = jnp.sum(picked * route_gates[:, :, None], axis=1)
    return mixed.astype(jnp.bfloat16)


def solution(mesh):
    placed = (
        P(("dp", "expert"), "tensor"),
        P(("dp", "expert"), None),
        P(("dp", "expert"), None),
        P("expert", None, "tensor"),
        P("expert", None, "tensor"),
        P("expert", "tensor", None),
    )
    return jax.shard_map(
        body, mesh=mesh, in_specs=placed, out_specs=P(("dp", "expert"), "tensor"), check_vma=False
    )
```

profile of v0, /device:TPU:0, one launch (start us, length us, event | category | flops | bytes accessed | tf_op | source)
XLA Modules:
  0.0 282.4 jit_solution(8101262847428519294)
XLA Ops:
  6.5 0.0 all-gather.2.cloned.1.call-start
  6.5 0.8 copy.9
  7.4 0.2 eq.26
  7.5 0.2 reshape.107
  7.7 0.6 reduce-window.6
  8.3 0.2 slice_reduce_fusion
  8.5 0.2 reduce-window.9
  8.7 0.1 add_bitcast_fusion
  8.8 0.2 reduce_sum.23
  9.0 0.1 compare_and_fusion
  9.2 0.2 lt.47
  9.4 0.2 mul.40
  9.6 3.0 %broadcast_in_dim.29 = bf16[512,2,1536]{2,1,0:T(2,128)(2,1)S(1)} broadcast(bf16[512,1536]{1,0:T(8,128)(2,1)} %param.6), dimensions={0,2} | broadcast | bytes 4718592 | tf_op jit(solution)/shard_map/broadcast_in_dim | solution.py:20
  12.6 2.7 reshape.128
  15.3 6.7 %scatter_custom_fusion = bf16[512,1536]{1,0:T(8,128)(2,1)S(1)} fusion(s32[1024]{0:T(1024)S(1)} %bitcast.73, bf16[1024,1536]{1,0:T(8,128)(2,1)} %reshape.128, bf16[]{:T(256)} %constant.17.clone.1), kind=kCustom, calls=%fused_computation.15 | custom fusion | bytes 1573376 | tf_op jit(solution)/shard_map/scatter | solution.py:24
  22.0 5.8 %all_to_all.10 = bf16[2,256,1536]{2,1,0:T(8,128)(2,1)} all-to-all(bf16[2,256,1536]{2,1,0:T(8,128)(2,1)S(1)} %bitcast.71), channel_id=1, replica_groups=mesh['dp'=4,'expert'=2,'tensor'=4] {'expert'}, dimensions={0} | all-to-all | bytes 3145728 | tf_op jit(solution)/shard_map/all_to_all | solution.py:27
  27.9 0.0 all-gather.2.cloned.1.call-update
  27.9 0.2 reduce-scatter.2.cloned.1.call-start
  28.1 72.8 %all-gather.2.cloned.1.call-done = bf16[2,256,6144]{2,1,0:T(8,128)(2,1)} async-done(((bf16[2,256,1536]{2,1,0:T(8,128)(2,1)}), bf16[2,256,6144]{2,1,0:T(8,128)(2,1)}) %all-gather.2.cloned.1.call-update) | async-done | bytes 6291472 | tf_op jit(solution)/shard_map/all_gather | solution.py:28
  100.9 0.0 copy-start.1
  100.9 0.0 slice-start
  100.9 8.1 %fusion.6 = f32[2,1,256,512]{3,2,0,1:T(8,128)S(1)} fusion(bf16[2,256,6144]{2,1,0:T(8,128)(2,1)} %all-gather.2.cloned.1.call-done, bf16[1,6144,512]{2,1,0:T(8,128)(2,1)} %param.9), kind=kOutput, calls=%fused_computation.10 | convolution fusion | flops 3221225472 | bytes 13631488 | tf_op jit(solution)/shard_map/secd,edf->secf/dot_general | solution.py:31
  109.0 0.0 copy-done.1
  109.0 0.0 slice-start.1
  109.0 6.5 %fusion.18 = bf16[2,256,512]{2,1,0:T(8,128)(2,1)S(1)} fusion(bf16[2,256,6144]{2,1,0:T(8,128)(2,1)S(1)} %copy-done.1, bf16[1,6144,512]{2,1,0:T(8,128)(2,1)} %param.10, f32[2,1,256,512]{3,2,0,1:T(8,128)S(1)} %fusion.6), kind=kOutput, calls=%fused_computation.14 | convolution fusion | flops 3222798336 | bytes 14155776 | tf_op jit(solution)/shard_map/secd,edf->secf/dot_general | solution.py:32
  115.5 0.0 slice-done
  115.5 0.0 slice-done.1
  115.6 6.4 %fusion = f32[2,256,6144]{2,1,0:T(8,128)} fusion(bf16[2,256,512]{2,1,0:T(8,128)(2,1)S(1)} %fusion.18, bf16[1,512,6144]{2,1,0:T(8,128)(2,1)S(1)} %bitcast.70), kind=kOutput, calls=%fused_computation.2 | convolution fusion | flops 3221225472 | bytes 19398656 | tf_op jit(solution)/shard_map/secf,efd->secd/dot_general | solution.py:34
  122.0 0.0 copy-start
  122.0 0.0 reduce-scatter.2.cloned.1.call-update
  122.0 0.7 copy-done
  122.7 0.1 copy.13
  122.8 120.1 %reduce-scatter.2.cloned.1.call-done = f32[2,256,1536]{2,1,0:T(8,128)} async-done(((f32[2,256,6144]{2,1,0:T(8,128)}), f32[2,256,1536]{2,1,0:T(8,128)}) %reduce-scatter.2.cloned.1.call-update) | async-done | bytes 3145744 | tf_op jit(solution)/shard_map/reduce_scatter | solution.py:36
  242.9 2.1 convert_element_type.23
  245.0 5.0 %all_to_all.11 = bf16[2,256,1536]{2,1,0:T(8,128)(2,1)S(1)} all-to-all(bf16[2,256,1536]{2,1,0:T(8,128)(2,1)S(1)} %convert_element_type.23), channel_id=1, replica_groups=mesh['dp'=4,'expert'=2,'tensor'=4] {'expert'}, dimensions={0} | all-to-all | bytes 3145728 | tf_op jit(solution)/shard_map/all_to_all | solution.py:38
  250.0 5.6 %gather_fusion = bf16[1024,1536]{1,0:T(8,128)(2,1)} fusion(bf16[512,1536]{1,0:T(8,128)(2,1)S(1)} %bitcast.68, s32[1024]{0:T(1024)S(1)} %broadcast_clamp_fusion), kind=kCustom, calls=%fused_computation | custom fusion | bytes 6295552 | tf_op jit(solution)/shard_map/jit(_take)/gather | solution.py:40
  255.6 6.0 %gather.7 = bf16[512,2,1536]{2,1,0:T(2,128)(2,1)S(1)} reshape(bf16[1024,1536]{1,0:T(8,128)(2,1)} %gather_fusion) | data formatting | bytes 6291456 | tf_op jit(solution)/shard_map/jit(_take)/gather | solution.py:40
  261.6 13.9 %multiply_reduce_fusion = bf16[512,1536]{1,0:T(8,128)(2,1)} fusion(bf16[512,2,1536]{2,1,0:T(2,128)(2,1)S(1)} %gather.7, pred[512,2]{1,0:T(8,128)(4,1)S(1)} %get-tuple-element.5, f32[512,2]{1,0:T(8,128)S(1)} %copy.13), kind=kLoop, calls=%fused_computation.8 | loop fusion | flops 5505024 | bytes 4723712 | tf_op jit(solution)/shard_map/reduce_sum | solution.py:42
  (6 shorter events, 0.1 us)
Async XLA Ops:
  6.5 94.4 %all-gather.2.cloned.1.call-start = ((), (), s32[]{:S(2)}) async-start(), calls=%async_computation.3 | async-start | bytes 7864320 | tf_op jit(solution)/shard_map/all_gather | solution.py:28
  27.9 215.0 %reduce-scatter.2.cloned.1.call-start = ((), (), s32[]{:S(2)}) async-start(), calls=%async_computation.4 | async-start | bytes 15728640 | tf_op jit(solution)/shard_map/reduce_scatter | solution.py:36
  100.9 8.1 %copy-start.1 = (bf16[2,256,6144]{2,1,0:T(8,128)(2,1)S(1)}, bf16[2,256,6144]{2,1,0:T(8,128)(2,1)}, u32[]{:S(2)}) copy-start(bf16[2,256,6144]{2,1,0:T(8,128)(2,1)} %all-gather.2.cloned.1.call-done) | copy-start | bytes 18874372
  100.9 14.6 %slice-start = ((s8[6291456]{0:T(1024)(128)(4,1)}), s8[4194304]{0:T(1024)(128)(4,1)S(1)}, s32[]{:S(2)}) async-start(s8[6291456]{0:T(1024)(128)(4,1)} %bitcast.69), calls=%async_computation.5 | async-start | bytes 8388608
  109.0 6.5 %slice-start.1 = ((s8[6291456]{0:T(1024)(128)(4,1)}), s8[2097152]{0:T(1024)(128)(4,1)S(1)}, s32[]{:S(2)}) async-start(s8[6291456]{0:T(1024)(128)(4,1)} %bitcast.69), calls=%async_computation.6 | async-start | bytes 4194304
  122.0 0.7 copy-start
Sparse Core Ops, SparseCore 0:
  28.0 72.8 all-gather.1
  122.1 120.7 reduce-scatter.1
where the time goes:
time: 283 us; the launch traced here: 282 us
  waiting for transfers between devices  193 us (68%)
  local copies, waits for them, and re-layouts  26.8 us (9%)
  matrix products  21 us (7%)
  other arithmetic  17.1 us (6%)
  between operations  13.6 us (5%)
  blocking collectives  10.8 us (4%)
    reduce_scatter x1, waiting for transfers between devices, body(): lax.psum_scatter(partial_out, 'tensor', scatter_dimension=2, tiled=True)  120 us
    all_gather x1, waiting for transfers between devices, body(): piece = lax.all_gather(received, 'tensor', axis=2, tiled=True)  72.8 us
    reduce_sum x1, other arithmetic, body(): mixed = jnp.sum(picked * route_gates[:, :, None], axis=1)  13.9 us
    gather x2, local copies, waits for them, and re-layouts, body(): jnp.take(flat_back, slots, axis=0, mode='fill', fill_value=0)  11.6 us
    dot_general x1, matrix products, body(): jnp.einsum('secd,edf->secf', grouped, w_gate, preferred_element_type=jnp....  8.11 us
    scatter x1, local copies, waits for them, and re-layouts, body(): buffer = jnp.zeros((n_flight * capacity, width_dev), jnp.bfloat16).at[slo...  6.69 us
    dot_general x1, matrix products, body(): jnp.einsum('secd,edf->secf', grouped, w_up, preferred_element_type=jnp.fl...  6.48 us
    dot_general x1, matrix products, body(): jnp.einsum('secf,efd->secd', gated, w_down, preferred_element_type=jnp.fl...  6.42 us
  transfers between devices with their start and end apart: 2, of which 2 were waited for; matrix products, arithmetic and copies ran while one was open for 0% of the time, Pallas kernels for 0%

commit v1 on v0

--- a/solution.py
+++ b/solution.py
@@ -1,10 +1,344 @@
+import functools
+
 import jax
 import jax.numpy as jnp
 from jax import lax
+from jax.experimental import pallas as pl
+from jax.experimental.pallas import tpu as pltpu
 from jax.sharding import PartitionSpec as P
 
-
-def body(tokens, route_ids, route_gates, w_gate, w_up, w_down):
+MESH = pl.DeviceIdType.MESH
+AG1X, AG1Y, AG2X, AG2Y, RS1X, RS1Y, RS2X, RS2Y, RET = range(9)
+
+
+def moe_kernel(
+    rows_full,
+    chunk,
+    ahead,
+    tok_ref,
+    idr_ref,
+    idc_ref,
+    gat_ref,
+    wg_hbm,
+    wu_hbm,
+    wd_hbm,
+    out_ref,
+    xg,
+    wg,
+    wu,
+    wd,
+    dsp,
+    snd_d,
+    snd_x,
+    snd_y,
+    got_d,
+    got_x,
+    got_y,
+    own,
+    back,
+    ret,
+    pt_own,
+    pt_oth,
+    send_sem,
+    recv_sem,
+    wsem,
+    dsem,
+):
+    cap = rows_full
+    tok_rows, width = tok_ref.shape
+    nch = 2 * cap // chunk
+    half_ch = nch // 2
+    hc = chunk // 2
+    e = lax.axis_index("expert")
+    t = lax.axis_index("tensor")
+    tx = (t // 2) * 2 + (1 - t % 2)
+    ty = (1 - t // 2) * 2 + t % 2
+    td = 3 - t
+
+    barrier = pltpu.get_barrier_semaphore()
+    pl.semaphore_signal(barrier, inc=1, device_id={"expert": 1 - e}, device_id_type=MESH)
+    pl.semaphore_signal(barrier, inc=1, device_id={"tensor": tx}, device_id_type=MESH)
+    pl.semaphore_signal(barrier, inc=1, device_id={"tensor": ty}, device_id_type=MESH)
+
+    def weight_copies():
+        copies = [
+            pltpu.make_async_copy(wg_hbm, wg, wsem.at[0]),
+            pltpu.make_async_copy(wu_hbm, wu, wsem.at[1]),
+        ]
+        for s in range(4):
+            copies.append(
+                pltpu.make_async_copy(
+                    wd_hbm.at[:, pl.ds(s * width, width)], wd.at[s], wsem.at[2 + s]
+                )
+            )
+        return copies
+
+    for c in weight_copies():
+        c.start()
+
+    def rows(k):
+        return pl.ds(pl.multiple_of(k * chunk, chunk), chunk)
+
+    def first(k):
+        return pl.ds(pl.multiple_of(k * chunk, hc), hc)
+
+    def second(k):
+        return pl.ds(pl.multiple_of(k * chunk + hc, hc), hc)
+
+    def remote(kind, k, src, dst, device):
+        return pltpu.make_async_remote_copy(
+            src_ref=src,
+            dst_ref=dst,
+            send_sem=send_sem.at[kind, k],
+            recv_sem=recv_sem.at[kind, k],
+            device_id=device,
+            device_id_type=MESH,
+        )
+
+    to_x, to_y, to_p = {"tensor": tx}, {"tensor": ty}, {"expert": 1 - e}
+
+    def ag1x(k):
+        return remote(AG1X, k, xg.at[t, rows(k)], xg.at[t, rows(k)], to_x)
+
+    def ag1y(k):
+        return remote(AG1Y, k, xg.at[t, rows(k)], xg.at[t, rows(k)], to_y)
+
+    def ag2x(k):
+        return remote(AG2X, k, xg.at[ty, second(k)], xg.at[ty, second(k)], to_x)
+
+    def ag2y(k):
+        return remote(AG2Y, k, xg.at[tx, first(k)], xg.at[tx, first(k)], to_y)
+
+    def rs1x(k):
+        return remote(RS1X, k, snd_d.at[first(k)], got_d.at[first(k)], to_x)
+
+    def rs1y(k):
+        return remote(RS1Y, k, snd_d.at[second(k)], got_d.at[second(k)], to_y)
+
+    def rs2x(k):
+        return remote(RS2X, k, snd_x.at[rows(k)], got_x.at[rows(k)], to_x)
+
+    def rs2y(k):
+        return remote(RS2Y, k, snd_y.at[rows(k)], got_y.at[rows(k)], to_y)
+
+    def give(k):
+        return remote(RET, k, ret.at[rows(k)], back.at[1, rows(k)], to_p)
+
+    dispatch = pltpu.make_async_remote_copy(
+        src_ref=dsp,
+        dst_ref=xg.at[t, pl.ds(cap, cap)],
+        send_sem=dsem.at[0],
+        recv_sem=dsem.at[1],
+        device_id=to_p,
+        device_id_type=MESH,
+    )
+
+    before = (
+        lax.broadcasted_iota(jnp.int32, (tok_rows, tok_rows), 0)
+        < lax.broadcasted_iota(jnp.int32, (tok_rows, tok_rows), 1)
+    )
+    before = jnp.where(before, 1.0, 0.0).astype(jnp.bfloat16)
+
+    def onehot(expert):
+        named = (idr_ref[0:1, :] == expert) | (idr_ref[1:2, :] == expert)
+        named = jnp.where(named, 1.0, 0.0)
+        wide = jnp.broadcast_to(named, (16, tok_rows)).astype(jnp.bfloat16)
+        pos = jnp.dot(wide, before, preferred_element_type=jnp.float32)[0:1, :]
+        pos = jnp.where(named > 0.5, pos, -1.0).astype(jnp.int32)
+        slot = lax.broadcasted_iota(jnp.int32, (cap, tok_rows), 0)
+        return jnp.where(slot == pos, 1.0, 0.0)
+
+    tok = tok_ref[...]
+    pick_own = onehot(e)
+    xg[t, 0:cap] = jnp.dot(
+        pick_own.astype(jnp.bfloat16), tok, preferred_element_type=jnp.float32
+    ).astype(jnp.bfloat16)
+    pl.semaphore_wait(barrier, 3)
+    for k in range(min(ahead, half_ch)):
+        ag1x(k).start()
+        ag1y(k).start()
+    pick_oth = onehot(1 - e)
+    dsp[...] = jnp.dot(
+        pick_oth.astype(jnp.bfloat16), tok, preferred_element_type=jnp.float32
+    ).astype(jnp.bfloat16)
+    dispatch.start()
+    pt_own[...] = pick_own.T.astype(jnp.bfloat16)
+    pt_oth[...] = pick_oth.T.astype(jnp.bfloat16)
+
+    def step(i, carry):
+        @pl.when(i + ahead == half_ch)
+        def _():
+            dispatch.wait_recv()
+
+        @pl.when(i + ahead < nch)
+        def _():
+            ag1x(i + ahead).start()
+            ag1y(i + ahead).start()
+
+        @pl.when(i < nch)
+        def _():
+            ag1x(i).wait_recv()
+            ag2y(i).start()
+            ag1y(i).wait_recv()
+            ag2x(i).start()
+
+        @pl.when(i == 1)
+        def _():
+            for c in weight_copies():
+                c.wait()
+
+        @pl.when((i >= 1) & (i - 1 < nch))
+        def _():
+            k = i - 1
+            ag2x(k).wait_recv()
+            ag2y(k).wait_recv()
+            gate = jnp.zeros((chunk, wg.shape[2]), jnp.float32)
+            upper = gate
+            for s in range(4):
+                part = xg[s, rows(k), :]
+                gate += jnp.dot(part, wg[s], preferred_element_type=jnp.float32)
+                upper += jnp.dot(part, wu[s], preferred_element_type=jnp.float32)
+            gated = (gate / (1.0 + jnp.exp(-gate)) * upper).astype(jnp.bfloat16)
+            snd_d[rows(k), :] = jnp.dot(
+                gated, wd[td], preferred_element_type=jnp.float32
+            ).astype(jnp.bfloat16)
+            rs1x(k).start()
+            rs1y(k).start()
+            snd_x[rows(k), :] = jnp.dot(
+                gated, wd[tx], preferred_element_type=jnp.float32
+            ).astype(jnp.bfloat16)
+            snd_y[rows(k), :] = jnp.dot(
+                gated, wd[ty], preferred_element_type=jnp.float32
+            ).astype(jnp.bfloat16)
+            own[rows(k), :] = jnp.dot(gated, wd[t], preferred_element_type=jnp.float32)
+
+        @pl.when((i >= 2) & (i - 2 < nch))
+        def _():
+            k = i - 2
+            rs1x(k).wait_recv()
+            snd_y[first(k), :] = (
+                snd_y[first(k), :].astype(jnp.float32) + got_d[first(k), :].astype(jnp.float32)
+            ).astype(jnp.bfloat16)
+            rs2y(k).start()
+            rs1y(k).wait_recv()
+            snd_x[second(k), :] = (
+                snd_x[second(k), :].astype(jnp.float32) + got_d[second(k), :].astype(jnp.float32)
+            ).astype(jnp.bfloat16)
+            rs2x(k).start()
+
+        @pl.when(i >= 3)
+        def _():
+            k = i - 3
+            rs2x(k).wait_recv()
+            rs2y(k).wait_recv()
+            done = (
+                own[rows(k), :]
+                + got_x[rows(k), :].astype(jnp.float32)
+                + got_y[rows(k), :].astype(jnp.float32)
+            ).astype(jnp.bfloat16)
+
+            @pl.when(k < half_ch)
+            def _():
+                back[0, rows(k), :] = done
+
+            @pl.when(k >= half_ch)
+            def _():
+                ret[rows(k - half_ch), :] = done
+                give(k - half_ch).start()
+
+        return carry
+
+    lax.fori_loop(0, nch + 3, step, 0)
+
+    def weight_of(expert):
+        ids = idc_ref[...]
+        gates = gat_ref[...]
+        return jnp.sum(jnp.where(ids == expert, gates, 0.0), axis=1, keepdims=True)
+
+    mine = weight_of(e) * jnp.dot(pt_own[...], back[0], preferred_element_type=jnp.float32)
+
+    def landed(k, carry):
+        give(k).wait_recv()
+        return carry
+
+    lax.fori_loop(0, half_ch, landed, 0)
+    theirs = weight_of(1 - e) * jnp.dot(pt_oth[...], back[1], preferred_element_type=jnp.float32)
+    out_ref[...] = (mine + theirs).astype(jnp.bfloat16)
+
+    dispatch.wait_send()
+
+    def drain(k, carry):
+        for make in (ag1x, ag1y, ag2x, ag2y, rs1x, rs1y, rs2x, rs2y):
+            make(k).wait_send()
+        return carry
+
+    lax.fori_loop(0, nch, drain, 0)
+
+    def drain_give(k, carry):
+        give(k).wait_send()
+        return carry
+
+    lax.fori_loop(0, half_ch, drain_give, 0)
+
+
+def fused(tokens, route_ids, route_gates, w_gate, w_up, w_down):
+    tok_rows, width = tokens.shape
+    tensor = lax.axis_size("tensor")
+    cap = tok_rows // 2
+    chunk = 128
+    ahead = 2
+    hidden = w_gate.shape[2]
+    total = 2 * cap
+    nch = total // chunk
+    bf16 = jnp.bfloat16
+    vmem = pl.BlockSpec(memory_space=pltpu.VMEM)
+    hbm = pl.BlockSpec(memory_space=pl.ANY)
+    flops = 2 * total * tensor * width * hidden * 3
+    return pl.pallas_call(
+        functools.partial(moe_kernel, cap, chunk, ahead),
+        out_shape=jax.ShapeDtypeStruct((tok_rows, width), bf16),
+        in_specs=[vmem, vmem, vmem, vmem, hbm, hbm, hbm],
+        out_specs=vmem,
+        scratch_shapes=[
+            pltpu.VMEM((tensor, total, width), bf16),
+            pltpu.VMEM((tensor, width, hidden), bf16),
+            pltpu.VMEM((tensor, width, hidden), bf16),
+            pltpu.VMEM((tensor, hidden, width), bf16),
+            pltpu.VMEM((cap, width), bf16),
+            pltpu.VMEM((total, width), bf16),
+            pltpu.VMEM((total, width), bf16),
+            pltpu.VMEM((total, width), bf16),
+            pltpu.VMEM((total, width), bf16),
+            pltpu.VMEM((total, width), bf16),
+            pltpu.VMEM((total, width), bf16),
+            pltpu.VMEM((total, width), jnp.float32),
+            pltpu.VMEM((2, cap, width), bf16),
+            pltpu.VMEM((cap, width), bf16),
+            pltpu.VMEM((tok_rows, cap), bf16),
+            pltpu.VMEM((tok_rows, cap), bf16),
+            pltpu.SemaphoreType.DMA((9, nch)),
+            pltpu.SemaphoreType.DMA((9, nch)),
+            pltpu.SemaphoreType.DMA((6,)),
+            pltpu.SemaphoreType.DMA((2,)),
+        ],
+        compiler_params=pltpu.CompilerParams(
+            collective_id=0, has_side_effects=True, vmem_limit_bytes=60 * 1024 * 1024
+        ),
+        cost_estimate=pl.CostEstimate(
+            flops=flops, bytes_accessed=3 * tensor * width * hidden * 2, transcendentals=0
+        ),
+    )(
+        tokens,
+        route_ids.T,
+        route_ids,
+        route_gates,
+        w_gate.reshape(tensor, width, hidden),
+        w_up.reshape(tensor, width, hidden),
+        w_down.reshape(hidden, tensor * width),
+    )
+
+
+def general(tokens, route_ids, route_gates, w_gate, w_up, w_down):
     tok_rows, width_dev = tokens.shape
     picks = route_ids.shape[1]
     n_source = lax.axis_size("expert")
@@ -52,6 +386,11 @@
         P("expert", None, "tensor"),
         P("expert", "tensor", None),
     )
+    square = mesh.shape["tensor"] == 4 and mesh.shape["expert"] == 2
     return jax.shard_map(
-        body, mesh=mesh, in_specs=placed, out_specs=P(("dp", "expert"), "tensor"), check_vma=False
-    )
+        fused if square else general,
+        mesh=mesh,
+        in_specs=placed,
+        out_specs=P(("dp", "expert"), "tensor"),
+        check_vma=False,
+    )

time: 283 us -> 118 us (0.42)
  waiting for transfers between devices: 193 us -> 0 us
  Pallas kernels: 0 us -> 111 us
  local copies, waits for them, and re-layouts: 26.8 us -> 5.73 us
  matrix products: 21 us -> 0 us
  other arithmetic: 17.1 us -> 0 us
  between operations: 13.6 us -> 0.01 us
  blocking collectives: 10.8 us -> 0 us
    reduce_scatter x1 -> x0, waiting for transfers between devices: 120 us -> none  [body(): lax.psum_scatter(partial_out, 'tensor', scatter_dimension=2, tiled=True)]
    pallas_call x0 -> x1, Pallas kernels: none -> 111 us  [fused(): pl.pallas_call(functools.partial(moe_kernel, cap, chunk, ahead), out_shap...]
    all_gather x1 -> x0, waiting for transfers between devices: 72.8 us -> none  [body(): piece = lax.all_gather(received, 'tensor', axis=2, tiled=True)]
    dot_general x3 -> x0, matrix products: 21 us -> none  [the longest x1 8.11 us: body(): jnp.einsum('secd,edf->secf', grouped, w_gate, preferred_element_type=jnp....]
    reduce_sum x2 -> x0, other arithmetic: 14 us -> none  [the longest x1 13.9 us: body(): mixed = jnp.sum(picked * route_gates[:, :, None], axis=1)]
    gather x2 -> x0, local copies, waits for them, and re-layouts: 11.6 us -> none  [body(): jnp.take(flat_back, slots, axis=0, mode='fill', fill_value=0)]
    all_to_all x2 -> x0, blocking collectives: 10.8 us -> none  [the longest x1 5.84 us: body(): lax.all_to_all(buffer, 'expert', split_axis=0, concat_axis=0, tiled=True)]
    scatter x1 -> x0, local copies, waits for them, and re-layouts: 6.69 us -> none  [body(): buffer = jnp.zeros((n_flight * capacity, width_dev), jnp.bfloat16).at[slo...]
  transfers between devices with their start and end apart: 2 -> 0, of which waited for: 2 -> 0; matrix products, arithmetic and copies ran while one was open for 0% -> 0% of each run, Pallas kernels for 0% -> 0%
where the time goes in v1:
time: 118 us; the launch traced here: 117 us
  Pallas kernels  111 us (94%)
  local copies, waits for them, and re-layouts  5.73 us (5%)
    pallas_call x1, Pallas kernels, fused(): pl.pallas_call(functools.partial(moe_kernel, cap, chunk, ahead), out_shap...  111 us
    unnamed x3, local copies, waits for them, and re-layouts  5.73 us

profile of v1, /device:TPU:0, one launch (start us, length us, event | category | flops | bytes accessed | tf_op | source)
XLA Modules:
  0.0 116.7 jit_solution(14506668843879570034)
XLA Ops:
  0.0 1.5 %copy.8.gat_ref = f32[512,2]{1,0:T(8,128)} copy(f32[512,2]{0,1:T(2,128)} %param.8) | data formatting | bytes 8192 | tf_op args[2]
  1.5 1.5 %copy.7.idc_ref = s32[512,2]{1,0:T(8,128)} copy(s32[512,2]{0,1:T(2,128)} %param.7) | data formatting | bytes 8192 | tf_op args[1]
  3.1 111.0 %shard_map.64 = bf16[512,1536]{1,0:T(8,128)(2,1)} custom-call(bf16[512,1536]{1,0:T(8,128)(2,1)} %tok_ref.1, s32[2,512]{1,0:T(2,128)} %bitcast.4, s32[512,2]{1,0:T(8,128)} %copy.7.idc_ref, f32[512,2]{1,0:T(8,128)} %copy.8.gat_ref, bf16[4,1536,512]{2,1,0:T(8,128)(2,1)} %bitcast.5, bf16[4,1536,512]{2,1,0:T(8,128)(2,1)} %bitcast.6, bf16[512,6144]{1,0:T(8,128)(2,1)} %bitcast.7), custom_call_target="tpu_custom_call" | custom-call | flops 9663676416 | bytes 18874368 | tf_op jit(solution)/shard_map/pallas_call | solution.py:297
  114.1 2.7 %copy.10 = bf16[512,1536]{1,0:T(8,128)(2,1)} copy(bf16[512,1536]{1,0:T(8,128)(2,1)} %shard_map.64) | data formatting | bytes 3145728
